TPU v7x, 32 devices: a whole 2x2x4 slice. The times are simulated.
32 devices in a mesh: wide: 8 (over z, x), narrow: 4 (over y, core).
Axes of the slice: x: 2, y: 2, z: 4, core: 2. Of those that a mesh axis runs over, the one named last changes fastest.
Arguments:
- state: float32 [4, 512, 512], P('narrow'), may hold values from -1.5 to 1.5
- left_env: float32 [32, 4, 512, 512], P('wide', 'narrow')
- right_env: float32 [32, 4, 512, 512], P('wide', 'narrow')
- left_sizes: int32 [4], replicated, may hold values from 1 to 512, 1536 in all
- right_sizes: int32 [4], replicated, may hold values from 1 to 512, 1536 in all
- channel_charge: int32 [32], P('wide'), may hold values from 0 to 2
Outputs:
- lanczos_vector: float32 [4, 512, 512], P('narrow', 'wide')
- alpha: float32 [], replicated
Inputs may be any that keep to these rules, and one draw needn't show every extreme that they name: `left_sizes`: basis states of each left sector; they add up to 1536, and some sector has exactly 512. `right_sizes`: basis states of each right sector; they add up to 1536, and some sector has exactly 512. `channel_charge`: 0 lowers the sector by one, 1 keeps it, 2 raises it by one.
All inputs are finite; a program needn't handle non-finite values.
Results may differ from a plain program's by a relative error of at most 0.0003.
Values sent between devices are 32-bit elements; how exact they have to be, the bound alone decides.
No kernel may reach another device: no remote copies, remote signals or barrier semaphores. Data moves between devices by JAX's collectives and lax.ppermute only.
A program may use at most 64 MiB of HBM per device.

v0:
```python
import functools

import jax
import jax.numpy as jnp
from jax import lax
from jax.experimental import pallas as pl
from jax.experimental.pallas import tpu as pltpu
from jax.sharding import PartitionSpec as P

F32 = jnp.float32
BF16 = jnp.bfloat16
NN = (((1,), (0,)), ((), ()))
NT = (((1,), (1,)), ((), ()))
VMEM = pl.BlockSpec(memory_space=pltpu.VMEM)
HBM = pl.BlockSpec(memory_space=pltpu.HBM)
OWN, NEAR, FAR, NONE = range(4)
TAIL = 8


def split(value):
    high = value.astype(BF16)
    low = (value - high.astype(F32)).astype(BF16)
    return high, low


def product(left, right, dims):
    (lh, ll), (rh, rl) = left, right
    dot = functools.partial(lax.dot_general, dimension_numbers=dims, preferred_element_type=F32)
    return dot(lh, rh) + (dot(lh, rl) + dot(ll, rh))


def keep(value, rows, cols, first_row=0):
    row = lax.broadcasted_iota(jnp.int32, value.shape, 0) + first_row
    col = lax.broadcasted_iota(jnp.int32, value.shape, 1)
    return jnp.where((row < rows) & (col < cols), value, 0.0)


def band_order(n_wide):
    groups = min(4, n_wide)
    return [s + groups * t for s in range(groups) for t in range(n_wide // groups)]


def main_kernel(
    lsz, rsz, charge, state, left, right, near,
    table, psi, psi_band, norm, lh, ll, rh, rl, total,
    ls, rs, cs, lbuf, rbuf, sbuf, ph, pl_, sems, more,
):
    chans, block = left.shape[0], state.shape[1]
    me, here = lax.axis_index("narrow"), lax.axis_index("wide")
    count = ls.shape[0]
    small = [
        pltpu.make_async_copy(src, dst, more.at[i])
        for i, (src, dst) in enumerate(((lsz, ls), (rsz, rs), (charge, cs)))
    ]
    whole = pltpu.make_async_copy(state.at[0], sbuf, more.at[3])
    for copy in small + [whole]:
        copy.start()
    for copy in small:
        copy.wait()

    side = 1 - 2 * lax.rem(me, 2)
    sectors = (me, me + side, me - side)

    def size_at(sizes, sector):
        inside = (sector >= 0) & (sector < count)
        return jnp.where(inside, sizes[jnp.clip(sector, 0, count - 1)], 0)

    lcounts = [size_at(ls, sector) for sector in sectors] + [0]
    rcounts = [size_at(rs, sector) for sector in sectors] + [0]

    def pick(values, kind):
        found = values[NONE]
        for i in (OWN, NEAR, FAR):
            found = jnp.where(kind == i, values[i], found)
        return found

    kinds = []
    for c in range(chans):
        src = me - (cs[c] - 1)
        kind = jnp.where(src == me, OWN, jnp.where(src == sectors[NEAR], NEAR, FAR))
        kinds.append(jnp.where((src >= 0) & (src < count), kind, NONE))
    places = [
        sum((kinds[o] < kinds[c]).astype(jnp.int32) for o in range(chans))
        + sum((kinds[o] == kinds[c]).astype(jnp.int32) for o in range(c))
        for c in range(chans)
    ]
    copies = []
    for j in range(chans):
        chan = sum(jnp.where(places[c] == j, c, 0) for c in range(chans))
        copies.append(
            (
                pltpu.make_async_copy(right.at[chan, 0], rbuf.at[j], sems.at[0, j]),
                pltpu.make_async_copy(left.at[chan, 0], lbuf.at[j], sems.at[1, j]),
            )
        )
        for copy in copies[-1]:
            copy.start()

    n_close = sum((k <= NEAR).astype(jnp.int32) for k in kinds)
    n_far = sum((k == FAR).astype(jnp.int32) for k in kinds)
    place = lax.broadcasted_iota(jnp.int32, table.shape, 1)
    entries = jnp.where(place == 0, lcounts[FAR], jnp.where(place == 1, rcounts[FAR], 0))
    table[...] = jnp.where(place == 2, n_close, jnp.where(place == 3, n_close + n_far, entries))

    order = band_order(lax.axis_size("wide"))
    band = psi_band.shape[0]
    starts = [pl.multiple_of((here ^ shift) * band, band) for shift in order]

    total[...] = jnp.zeros_like(total)
    ph[NEAR], pl_[NEAR] = split(keep(near[...], lcounts[NEAR], rcounts[NEAR]))
    whole.wait()
    masked = keep(sbuf[...], lcounts[OWN], rcounts[OWN])
    ph[OWN], pl_[OWN] = split(masked)
    norm[...] = jnp.full(norm.shape, jnp.sum(masked * masked), F32)
    sbuf[...] = masked
    psi_band[...] = sbuf[pl.ds(pl.multiple_of(here * band, band), band), :]
    for p, start in enumerate(starts):
        psi[p * band : (p + 1) * band, :] = sbuf[pl.ds(start, band), :]

    for j in range(chans):
        kind = sum(jnp.where(places[c] == j, kinds[c], 0) for c in range(chans))
        lcount, rcount = pick(lcounts, kind), pick(rcounts, kind)
        for copy in copies[j]:
            copy.wait()

        def halve():
            rh[j], rl[j] = split(keep(rbuf[j], rcounts[OWN], rcount))
            for p, start in enumerate(starts):
                rows = slice(p * band, (p + 1) * band)
                piece = keep(lbuf[j, pl.ds(start, band), :], lcounts[OWN], lcount, start)
                lh[j, rows, :], ll[j, rows, :] = split(piece)

        @pl.when(kind <= NEAR)
        def _():
            halve()
            y = split(product((ph[kind], pl_[kind]), (rh[j], rl[j]), NT))
            total[...] += product((lh[j], ll[j]), y, NN)

        @pl.when(kind > NEAR)
        def _():
            halve()


def over_far(table, chans, group):
    first, have = table[0, 2], table[0, 3] - table[0, 2]
    for count in range(1, chans + 1):

        @pl.when(have == count)
        def _():
            group([first + i for i in range(count)])


def far_kernel(table, far, lh, ll, rh, rl, before, total, ph, pl_):
    rows = far.shape[0]

    @pl.when(table[0, 3] > table[0, 2])
    def _():
        ph[...], pl_[...] = split(keep(far[...], table[0, 0], table[0, 1]))

        def group(slots):
            psi = (ph[...], pl_[...])
            ys = [split(product(psi, (rh[j], rl[j]), NT)) for j in slots]
            terms = [product((lh[j, :, :rows], ll[j, :, :rows]), y, NN) for j, y in zip(slots, ys)]
            total[...] += functools.reduce(jnp.add, terms)

        over_far(table, lh.shape[0], group)


def last_kernel(table, far, lh, ll, rh, rl, before, psi, norm, *rest):
    *outs, total, ph, pl_ = rest
    rows = far.shape[0]
    block = psi.shape[0]
    total[...] = before[...]

    @pl.when(table[0, 3] > table[0, 2])
    def _():
        ph[...], pl_[...] = split(keep(far[...], table[0, 0], table[0, 1], block - rows))

        def group(slots):
            psi_far = (ph[...], pl_[...])
            ys = [split(product(psi_far, (rh[j], rl[j]), NT)) for j in slots]
            terms = [
                product((lh[j, :, block - rows :], ll[j, :, block - rows :]), y, NN) for j, y in zip(slots, ys)
            ]
            total[...] += functools.reduce(jnp.add, terms)

        over_far(table, lh.shape[0], group)

    row = lax.broadcasted_iota(jnp.int32, (TAIL, block), 0)
    sums = jnp.where(row == 0, jnp.sum(psi[...] * total[...]), norm[0, 0])
    size = outs[0].shape[0] - TAIL
    for i, out in enumerate(outs):
        out[:size, :] = total[i * size : (i + 1) * size, :]
        out[size:, :] = sums


def add_kernel(*refs):
    *parts, out = refs
    whole = parts[0][...]
    for part in parts[1:]:
        whole += part[...]
    out[...] = whole


def add_first_kernel(*refs):
    *parts, out = refs
    whole = parts[0][...]
    for part in parts[1:]:
        whole += part[...]
    row = lax.broadcasted_iota(jnp.int32, out.shape, 0)
    out[...] = jnp.where(row == 0, whole, parts[0][...])


def merge_kernel(*refs):
    *parts, sums, mine, give = refs
    half = mine.shape[0]
    whole = parts[0][: 2 * half, :]
    tail = parts[0][2 * half :, :128]
    first = tail
    for part in parts[1:]:
        whole += part[: 2 * half, :]
        first += part[2 * half :, :128]
    mine[...] = whole[:half]
    give[...] = whole[half:]
    row = lax.broadcasted_iota(jnp.int32, sums.shape, 0)
    sums[...] = jnp.where(row == 0, first, tail)


def halves_kernel(*refs):
    *parts, mine, give = refs
    half = mine.shape[0]
    whole = parts[0][...]
    for part in parts[1:]:
        whole += part[...]
    mine[...] = whole[:half]
    give[...] = whole[half:]


def final_kernel(n_parts, psi, *rest):
    parts, (*sums, out, alpha) = rest[:n_parts], rest[n_parts:]
    both = sums[0][0:2, :]
    for more in sums[1:]:
        both += more[0:2, :]
    ratio = both[0:1, :] / both[1:2, :]
    share = parts[0][...]
    for part in parts[1:]:
        share += part[...]
    out[...] = share - jnp.concatenate([ratio] * (psi.shape[1] // ratio.shape[1]), axis=1) * psi[...]
    alpha[...] = ratio


def exchange(value, axis, shift):
    count = lax.axis_size(axis)
    return lax.ppermute(value, axis, [(i, i ^ shift) for i in range(count)])


def f32(*shape):
    return jax.ShapeDtypeStruct(shape, F32)


def cost(flops, size=2**20):
    return pl.CostEstimate(flops=flops, bytes_accessed=size, transcendentals=0)


def call(kernel, out_shape, n_in, scratch=(), name=None, **more):
    return pl.pallas_call(
        kernel,
        out_shape=out_shape,
        in_specs=[VMEM] * n_in,
        out_specs=jax.tree.map(lambda _: VMEM, out_shape),
        scratch_shapes=scratch,
        compiler_params=pltpu.CompilerParams(vmem_limit_bytes=16 * 2**20),
        name=name,
        **more,
    )


def per_device(state, left_env, right_env, left_sizes, right_sizes, channel_charge):
    chans, _, block, _ = left_env.shape
    n_wide, n_narrow = lax.axis_size("wide"), lax.axis_size("narrow")
    band, half = block // n_wide, block // 2
    own = state[0]
    square, small = f32(block, block), f32(8, 128)
    work = 6 * chans * block**3

    ends = [(0, 0), (n_narrow - 1, n_narrow - 1)]
    across = [pair for k in range(1, n_narrow - 1, 2) for pair in ((k, k + 1), (k + 1, k))]
    far_top, far_low = (lax.ppermute(rows, "narrow", across + ends) for rows in (own[:half], own[half:]))
    near = exchange(own, "narrow", 1)

    halves = jax.ShapeDtypeStruct((chans, block, block), BF16)
    table, psi, psi_band, norm, lh, ll, rh, rl, total = pl.pallas_call(
        main_kernel,
        out_shape=[jax.ShapeDtypeStruct((8, 128), jnp.int32), square, f32(band, block), small]
        + [halves] * 4
        + [square],
        in_specs=[HBM] * 6 + [VMEM],
        out_specs=[VMEM] * 9,
        scratch_shapes=[
            pltpu.SMEM(left_sizes.shape, jnp.int32),
            pltpu.SMEM(right_sizes.shape, jnp.int32),
            pltpu.SMEM(channel_charge.shape, jnp.int32),
            pltpu.VMEM((chans, block, block), F32),
            pltpu.VMEM((chans, block, block), F32),
            pltpu.VMEM((block, block), F32),
            pltpu.VMEM((2, block, block), BF16),
            pltpu.VMEM((2, block, block), BF16),
            pltpu.SemaphoreType.DMA((2, chans)),
            pltpu.SemaphoreType.DMA((4,)),
        ],
        compiler_params=pltpu.CompilerParams(vmem_limit_bytes=32 * 2**20),
        cost_estimate=cost(work, 8 * chans * block * block),
        name="main",
    )(
        left_sizes, right_sizes, channel_charge,
        *(pltpu.with_memory_space_constraint(x, pltpu.HBM) for x in (state, left_env, right_env)),
        near,
    )
    envs = (lh, ll, rh, rl)

    pair = [pltpu.VMEM((half, block), BF16)] * 2
    total = call(far_kernel, square, 7, pair, name="far", cost_estimate=cost(work), input_output_aliases={6: 0})(table, far_top, *envs, total)

    groups = min(4, n_wide)
    held = n_wide // groups
    blocks = call(
        last_kernel, [f32(held * band + TAIL, block)] * groups, 9, [pltpu.VMEM((block, block), F32)] + pair,
        name="last", cost_estimate=cost(work),
    )(table, far_low, *envs, total, psi, norm)
    parts = [blocks[0]] + [exchange(blocks[s], "wide", s) for s in range(groups - 1, 0, -1)]

    held //= 2
    sums, mine, give = call(merge_kernel, [small] + [f32(held * band, block)] * 2, groups, name="merge")(*parts)
    step = groups
    while step < n_wide:
        sums = call(add_first_kernel, small, 2, name="wide", cost_estimate=cost(16 * block**3))(sums, exchange(sums, "wide", step))
        step *= 2
    parts = [mine, exchange(give, "wide", groups * held)]
    while held > 1:
        held //= 2
        mine, give = call(halves_kernel, [f32(held * band, block)] * 2, 2, name="halves")(*parts)
        parts = [mine, exchange(give, "wide", groups * held)]
    others = []
    if n_narrow <= 4:
        others = [exchange(sums, "narrow", s) for s in (1, 2, 3)]
    else:
        step = 1
        while step < n_narrow:
            sums = call(add_kernel, small, 2, name="sectors")(sums, exchange(sums, "narrow", step))
            step *= 2

    out, alpha = call(
        functools.partial(final_kernel, len(parts)), [f32(band, block), f32(1, 128)], 2 + len(parts) + len(others),
        name="final",
    )(psi_band, *parts, sums, *others)
    return out[None], alpha[0, 0]


def solution(mesh):
    placed = (
        P("narrow", None, None),
        P("wide", "narrow", None, None),
        P("wide", "narrow", None, None),
        P(),
        P(),
        P("wide"),
    )
    return jax.shard_map(
        per_device,
        mesh=mesh,
        in_specs=placed,
        out_specs=(P("narrow", "wide", None), P()),
        check_vma=False,
    )
```

profile of v0, /device:TPU:6, one launch (start us, length us, event | category | flops | bytes accessed | tf_op | source)
XLA Modules:
  0.0 43.1 jit_solution(14088840339919106648)
XLA Ops:
  0.6 0.0 copy-start.2
  0.6 0.0 copy-start.1
  0.7 0.0 copy-start
  0.7 0.1 collective-permute-start
  0.7 1.3 %slice_bitcast_fusion = (f32[256,512]{1,0:T(8,128)S(1)}, f32[256,512]{1,0:T(8,128)S(1)}) fusion(f32[1,512,512]{2,1,0:T(8,128)} %state.1), kind=kLoop, calls=%fused_computation | loop fusion | bytes 2097152 | tf_op jit(solution)/shard_map/slice | solution.py:288
  2.0 2.5 %collective-permute-start.2 = (f32[256,512]{1,0:T(8,128)S(1)}, f32[256,512]{1,0:T(8,128)S(1)}, u32[]{:S(2)}, u32[]{:S(2)}) collective-permute-start(f32[256,512]{1,0:T(8,128)S(1)} %get-tuple-element.38), channel_id=1, source_target_pairs={{1,2},{2,1},{0,0},{3,3},{5,6},{6,5},{4,4},{7,7},{9,10},{10,9},{8,8... | collective-permute-start | bytes 1572872 | tf_op jit(solution)/shard_map/ppermute | solution.py:288
  4.5 3.0 %collective-permute-start.1 = (f32[256,512]{1,0:T(8,128)S(1)}, f32[256,512]{1,0:T(8,128)S(1)}, u32[]{:S(2)}, u32[]{:S(2)}) collective-permute-start(f32[256,512]{1,0:T(8,128)S(1)} %get-tuple-element.39), channel_id=1, source_target_pairs={{1,2},{2,1},{0,0},{3,3},{5,6},{6,5},{4,4},{7,7},{9,10},{10,9},{8,8... | collective-permute-start | bytes 1572872 | tf_op jit(solution)/shard_map/ppermute | solution.py:288
  7.6 0.0 collective-permute-done.near
  7.6 0.0 copy-done.2
  7.6 0.0 copy-done.1
  7.6 0.0 copy-done
  7.6 8.8 %main.1 = (s32[8,128]{1,0:T(8,128)S(1)}, f32[512,512]{1,0:T(8,128)S(1)}, f32[64,512]{1,0:T(8,128)S(1)}, f32[8,128]{1,0:T(8,128)S(1)}, bf16[4,512,512]{2,1,0:T(8,...) custom-call(s32[4]{0:T(128)S(1)} %copy-done, ...), custom_call_target="tpu_custom_call" | custom-call | flops 3221225472 | bytes 8388608 | tf_op jit(solution)/shard_map/main/pallas_call | solution.py:292
  16.5 0.0 collective-permute-done.2.far
  16.5 1.9 %far.1.before = f32[512,512]{1,0:T(8,128)S(1)} custom-call(s32[8,128]{1,0:T(8,128)S(1)} %get-tuple-element.21.table, f32[256,512]{1,0:T(8,128)S(1)} %collective-permute-done.2.far, bf16[4,512,512]{2,1,0:T(8,128)(2,1)S(1)} %get-tuple-element.22.lh, bf16[4,512,512]{2,1,0:T(8,128)(2,1)S(1)} %get-tuple-element.23.ll, ...), custom_call_target="tpu_custom_call", output_to_operand_aliasing={{}: (6, {})} | custom-call | flops 3221225472 | bytes 1048576 | tf_op jit(solution)/shard_map/far/pallas_call | solution.py:322
  18.4 0.0 collective-permute-done.1.far
  18.4 1.9 %last.1 = (f32[136,512]{1,0:T(8,128)S(1)}, f32[136,512]{1,0:T(8,128)S(1)}, f32[136,512]{1,0:T(8,128)S(1)}, f32[136,512]{1,0:T(8,128)S(1)}) custom-call(s32[8,128]{1,0:T(8,128)S(1)} %get-tuple-element.21.table, f32[256,512]{1,0:T(8,128)S(1)} %collective-permute-done.1.far, bf16[4,512,512]{2,1,0:T(8,128)(2,1)S(1)} %get-tuple-element.22.lh, ...), custom_call_target="tpu_custom_call" | custom-call | flops 3221225472 | bytes 1048576 | tf_op jit(solution)/shard_map/last/pallas_call | solution.py:326
  20.4 2.0 %collective-permute-start.3 = (f32[136,512]{1,0:T(8,128)S(1)}, f32[136,512]{1,0:T(8,128)S(1)}, u32[]{:S(2)}, u32[]{:S(2)}) collective-permute-start(f32[136,512]{1,0:T(8,128)S(1)} %get-tuple-element.30), channel_id=1, source_target_pairs={{0,12},{4,8},{8,4},{12,0},{16,28},{20,24},{24,20},{28,16},{1,13},{... | collective-permute-start | bytes 835592 | tf_op jit(solution)/shard_map/ppermute | solution.py:254
  22.4 0.1 collective-permute-start.4
  22.4 1.5 %collective-permute-start.5 = (f32[136,512]{1,0:T(8,128)S(1)}, f32[136,512]{1,0:T(8,128)S(1)}, u32[]{:S(2)}, u32[]{:S(2)}) collective-permute-start(f32[136,512]{1,0:T(8,128)S(1)} %get-tuple-element.32), channel_id=1, source_target_pairs={{0,4},{4,0},{8,12},{12,8},{16,20},{20,16},{24,28},{28,24},{1,5},{5... | collective-permute-start | bytes 835592 | tf_op jit(solution)/shard_map/ppermute | solution.py:254
  23.9 4.1 %collective-permute-done.3.refs_1_ = f32[136,512]{1,0:T(8,128)S(1)} collective-permute-done((f32[136,512]{1,0:T(8,128)S(1)}, f32[136,512]{1,0:T(8,128)S(1)}, u32[]{:S(2)}, u32[]{:S(2)}) %collective-permute-start.3) | collective-permute-done | bytes 278560 | tf_op jit(solution)/shard_map/ppermute | solution.py:254
  28.0 3.4 %collective-permute-done.4.refs_2_ = f32[136,512]{1,0:T(8,128)S(1)} collective-permute-done((f32[136,512]{1,0:T(8,128)S(1)}, f32[136,512]{1,0:T(8,128)S(1)}, u32[]{:S(2)}, u32[]{:S(2)}) %collective-permute-start.4) | collective-permute-done | bytes 278560 | tf_op jit(solution)/shard_map/ppermute | solution.py:254
  31.4 0.0 collective-permute-done.5.refs_3_
  31.4 0.1 merge.1
  31.5 3.8 %collective-permute-start.7 = (f32[8,128]{1,0:T(8,128)S(1)}, f32[8,128]{1,0:T(8,128)S(1)}, u32[]{:S(2)}, u32[]{:S(2)}) collective-permute-start(f32[8,128]{1,0:T(8,128)S(1)} %get-tuple-element.35.refs_0_), channel_id=1, source_target_pairs={{0,16},{4,20},{8,24},{12,28},{16,0},{20,4},{24,8},{28,12},{1,17},{... | collective-permute-start | bytes 12296 | tf_op jit(solution)/shard_map/ppermute | solution.py:254
  35.3 0.1 collective-permute-start.6
  35.4 1.5 %collective-permute-done.7.refs_1_ = f32[8,128]{1,0:T(8,128)S(1)} collective-permute-done((f32[8,128]{1,0:T(8,128)S(1)}, f32[8,128]{1,0:T(8,128)S(1)}, u32[]{:S(2)}, u32[]{:S(2)}) %collective-permute-start.7) | collective-permute-done | bytes 4128 | tf_op jit(solution)/shard_map/ppermute | solution.py:254
  36.9 0.0 collective-permute-start.10
  36.9 0.1 collective-permute-start.9
  37.0 1.8 %collective-permute-start.8 = (f32[8,128]{1,0:T(8,128)S(1)}, f32[8,128]{1,0:T(8,128)S(1)}, u32[]{:S(2)}, u32[]{:S(2)}) collective-permute-start(f32[8,128]{1,0:T(8,128)S(1)} %wide.1.rest_2_), channel_id=1, source_target_pairs={{0,1},{1,0},{2,3},{3,2},{4,5},{5,4},{6,7},{7,6},{8,9},{9,8},{10,11... | collective-permute-start | bytes 12296 | tf_op jit(solution)/shard_map/ppermute | solution.py:254
  38.8 1.2 %collective-permute-done.10.rest_5_ = f32[8,128]{1,0:T(8,128)S(1)} collective-permute-done((f32[8,128]{1,0:T(8,128)S(1)}, f32[8,128]{1,0:T(8,128)S(1)}, u32[]{:S(2)}, u32[]{:S(2)}) %collective-permute-start.10) | collective-permute-done | bytes 4128 | tf_op jit(solution)/shard_map/ppermute | solution.py:254
  39.9 0.6 %collective-permute-done.9.rest_4_ = f32[8,128]{1,0:T(8,128)S(1)} collective-permute-done((f32[8,128]{1,0:T(8,128)S(1)}, f32[8,128]{1,0:T(8,128)S(1)}, u32[]{:S(2)}, u32[]{:S(2)}) %collective-permute-start.9) | collective-permute-done | bytes 4128 | tf_op jit(solution)/shard_map/ppermute | solution.py:254
  40.6 0.0 collective-permute-done.8.rest_3_
  40.6 1.8 %collective-permute-done.6.rest_1_ = f32[64,512]{1,0:T(8,128)S(1)} collective-permute-done((f32[64,512]{1,0:T(8,128)S(1)}, f32[64,512]{1,0:T(8,128)S(1)}, u32[]{:S(2)}, u32[]{:S(2)}) %collective-permute-start.6) | collective-permute-done | bytes 131104 | tf_op jit(solution)/shard_map/ppermute | solution.py:254
  42.4 0.7 %final.1 = (f32[64,512]{1,0:T(8,128)}, f32[1,128]{1,0:T(1,128)}) custom-call(f32[64,512]{1,0:T(8,128)S(1)} %get-tuple-element.20.psi, f32[64,512]{1,0:T(8,128)S(1)} %get-tuple-element.33.rest_0_, f32[64,512]{1,0:T(8,128)S(1)} %collective-permute-done.6.rest_1_, f32[8,128]{1,0:T(8,128)S(1)} %wide.1.rest_2_, f32[8,128]{1,0:T(8,128)S(1)} %collective-permute-done.8.rest_3_, ...), custom_call_target="tpu_custom_call" | custom-call | tf_op jit(solution)/shard_map/final/pallas_call | solution.py:352
  (1 shorter events, 0.0 us)
Async XLA Ops:
  0.6 7.0 %copy-start.2 = (s32[4]{0:T(128)S(1)}, s32[4]{0:T(128)}, u32[]{:S(2)}) copy-start(s32[4]{0:T(128)} %charge.1) | copy-start | bytes 52
  0.6 7.0 %copy-start.1 = (s32[4]{0:T(128)S(1)}, s32[4]{0:T(128)}, u32[]{:S(2)}) copy-start(s32[4]{0:T(128)} %rsz.1) | copy-start | bytes 52
  0.7 7.0 %copy-start = (s32[4]{0:T(128)S(1)}, s32[4]{0:T(128)}, u32[]{:S(2)}) copy-start(s32[4]{0:T(128)} %lsz.1) | copy-start | bytes 52
  0.7 6.9 %collective-permute-start = (f32[512,512]{1,0:T(8,128)}, f32[512,512]{1,0:T(8,128)S(1)}, u32[]{:S(2)}, u32[]{:S(2)}) collective-permute-start(f32[512,512]{1,0:T(8,128)} %bitcast.8), channel_id=1, source_target_pairs={{0,1},{1,0},{2,3},{3,2},{4,5},{5,4},{6,7},{7,6},{8,9},{9,8},{10,11... | collective-permute-start | bytes 3145736 | tf_op jit(solution)/shard_map/ppermute | solution.py:254
  2.0 14.5 %collective-permute-start.2 = (f32[256,512]{1,0:T(8,128)S(1)}, f32[256,512]{1,0:T(8,128)S(1)}, u32[]{:S(2)}, u32[]{:S(2)}) collective-permute-start(f32[256,512]{1,0:T(8,128)S(1)} %get-tuple-element.38), channel_id=1, source_target_pairs={{1,2},{2,1},{0,0},{3,3},{5,6},{6,5},{4,4},{7,7},{9,10},{10,9},{8,8... | collective-permute-start | bytes 1572872 | tf_op jit(solution)/shard_map/ppermute | solution.py:288
  4.5 13.9 %collective-permute-start.1 = (f32[256,512]{1,0:T(8,128)S(1)}, f32[256,512]{1,0:T(8,128)S(1)}, u32[]{:S(2)}, u32[]{:S(2)}) collective-permute-start(f32[256,512]{1,0:T(8,128)S(1)} %get-tuple-element.39), channel_id=1, source_target_pairs={{1,2},{2,1},{0,0},{3,3},{5,6},{6,5},{4,4},{7,7},{9,10},{10,9},{8,8... | collective-permute-start | bytes 1572872 | tf_op jit(solution)/shard_map/ppermute | solution.py:288
  20.4 7.6 %collective-permute-start.3 = (f32[136,512]{1,0:T(8,128)S(1)}, f32[136,512]{1,0:T(8,128)S(1)}, u32[]{:S(2)}, u32[]{:S(2)}) collective-permute-start(f32[136,512]{1,0:T(8,128)S(1)} %get-tuple-element.30), channel_id=1, source_target_pairs={{0,12},{4,8},{8,4},{12,0},{16,28},{20,24},{24,20},{28,16},{1,13},{... | collective-permute-start | bytes 835592 | tf_op jit(solution)/shard_map/ppermute | solution.py:254
  22.4 9.0 %collective-permute-start.4 = (f32[136,512]{1,0:T(8,128)S(1)}, f32[136,512]{1,0:T(8,128)S(1)}, u32[]{:S(2)}, u32[]{:S(2)}) collective-permute-start(f32[136,512]{1,0:T(8,128)S(1)} %get-tuple-element.31), channel_id=1, source_target_pairs={{0,8},{4,12},{8,0},{12,4},{16,24},{20,28},{24,16},{28,20},{1,9},{5... | collective-permute-start | bytes 835592 | tf_op jit(solution)/shard_map/ppermute | solution.py:254
  22.4 9.0 %collective-permute-start.5 = (f32[136,512]{1,0:T(8,128)S(1)}, f32[136,512]{1,0:T(8,128)S(1)}, u32[]{:S(2)}, u32[]{:S(2)}) collective-permute-start(f32[136,512]{1,0:T(8,128)S(1)} %get-tuple-element.32), channel_id=1, source_target_pairs={{0,4},{4,0},{8,12},{12,8},{16,20},{20,16},{24,28},{28,24},{1,5},{5... | collective-permute-start | bytes 835592 | tf_op jit(solution)/shard_map/ppermute | solution.py:254
  31.5 5.4 %collective-permute-start.7 = (f32[8,128]{1,0:T(8,128)S(1)}, f32[8,128]{1,0:T(8,128)S(1)}, u32[]{:S(2)}, u32[]{:S(2)}) collective-permute-start(f32[8,128]{1,0:T(8,128)S(1)} %get-tuple-element.35.refs_0_), channel_id=1, source_target_pairs={{0,16},{4,20},{8,24},{12,28},{16,0},{20,4},{24,8},{28,12},{1,17},{... | collective-permute-start | bytes 12296 | tf_op jit(solution)/shard_map/ppermute | solution.py:254
  35.3 7.1 %collective-permute-start.6 = (f32[64,512]{1,0:T(8,128)S(1)}, f32[64,512]{1,0:T(8,128)S(1)}, u32[]{:S(2)}, u32[]{:S(2)}) collective-permute-start(f32[64,512]{1,0:T(8,128)S(1)} %get-tuple-element.34), channel_id=1, source_target_pairs={{0,16},{4,20},{8,24},{12,28},{16,0},{20,4},{24,8},{28,12},{1,17},{... | collective-permute-start | bytes 393224 | tf_op jit(solution)/shard_map/ppermute | solution.py:254
  36.9 3.0 %collective-permute-start.10 = (f32[8,128]{1,0:T(8,128)S(1)}, f32[8,128]{1,0:T(8,128)S(1)}, u32[]{:S(2)}, u32[]{:S(2)}) collective-permute-start(f32[8,128]{1,0:T(8,128)S(1)} %wide.1.rest_2_), channel_id=1, source_target_pairs={{0,3},{1,2},{2,1},{3,0},{4,7},{5,6},{6,5},{7,4},{8,11},{9,10},{10,... | collective-permute-start | bytes 12296 | tf_op jit(solution)/shard_map/ppermute | solution.py:254
  36.9 3.7 %collective-permute-start.9 = (f32[8,128]{1,0:T(8,128)S(1)}, f32[8,128]{1,0:T(8,128)S(1)}, u32[]{:S(2)}, u32[]{:S(2)}) collective-permute-start(f32[8,128]{1,0:T(8,128)S(1)} %wide.1.rest_2_), channel_id=1, source_target_pairs={{0,2},{1,3},{2,0},{3,1},{4,6},{5,7},{6,4},{7,5},{8,10},{9,11},{10,... | collective-permute-start | bytes 12296 | tf_op jit(solution)/shard_map/ppermute | solution.py:254
  37.0 3.6 %collective-permute-start.8 = (f32[8,128]{1,0:T(8,128)S(1)}, f32[8,128]{1,0:T(8,128)S(1)}, u32[]{:S(2)}, u32[]{:S(2)}) collective-permute-start(f32[8,128]{1,0:T(8,128)S(1)} %wide.1.rest_2_), channel_id=1, source_target_pairs={{0,1},{1,0},{2,3},{3,2},{4,5},{5,4},{6,7},{7,6},{8,9},{9,8},{10,11... | collective-permute-start | bytes 12296 | tf_op jit(solution)/shard_map/ppermute | solution.py:254
where the time goes:
time: 43.5 us; the launch traced here: 43.1 us
  starting transfers between devices  15 us (34%)
  Pallas kernels  13.5 us (31%)
  waiting for transfers between devices  12.6 us (29%)
  local copies, waits for them, and re-layouts  1.28 us (3%)
  between operations  0.77 us (2%)
    ppermute x9, waiting for transfers between devices, exchange(): return lax.ppermute(value, axis, [(i, i ^ shift) for i in range(count)])  12.6 us
    ppermute x9, starting transfers between devices, exchange(): return lax.ppermute(value, axis, [(i, i ^ shift) for i in range(count)])  9.39 us
    pallas_call x1, Pallas kernels, per_device(): pl.pallas_call(main_kernel, out_shape=[jax.ShapeDtypeStruct((8, 128), jnp...  8.85 us
    ppermute x2, starting transfers between devices, per_device(): lax.ppermute(rows, 'narrow', across + ends)  5.56 us
    pallas_call x1, Pallas kernels, per_device(): call(far_kernel, square, 7, pair, name='far', cost_estimate=cost(work), i...  1.93 us
    pallas_call x1, Pallas kernels, per_device(): call(last_kernel, [f32(held * band + TAIL, block)] * groups, 9, [pltpu.VM...  1.92 us
    slice x1, local copies, waits for them, and re-layouts, per_device(): own[:half]  1.27 us
  transfers between devices with their start and end apart: 11, of which 6 were waited for; matrix products, arithmetic and copies ran while one was open for 3% of the time, Pallas kernels for 25%

commit v1 on v0

--- a/solution.py
+++ b/solution.py
@@ -170,7 +170,10 @@
     *outs, total, ph, pl_ = rest
     rows = far.shape[0]
     block = psi.shape[0]
-    total[...] = before[...]
+
+    @pl.when(table[0, 3] == table[0, 2])
+    def _():
+        total[...] = before[...]
 
     @pl.when(table[0, 3] > table[0, 2])
     def _():
@@ -182,7 +185,7 @@
             terms = [
                 product((lh[j, :, block - rows :], ll[j, :, block - rows :]), y, NN) for j, y in zip(slots, ys)
             ]
-            total[...] += functools.reduce(jnp.add, terms)
+            total[...] = before[...] + functools.reduce(jnp.add, terms)
 
         over_far(table, lh.shape[0], group)
 
@@ -341,13 +344,10 @@
         mine, give = call(halves_kernel, [f32(held * band, block)] * 2, 2, name="halves")(*parts)
         parts = [mine, exchange(give, "wide", groups * held)]
     others = []
-    if n_narrow <= 4:
-        others = [exchange(sums, "narrow", s) for s in (1, 2, 3)]
-    else:
-        step = 1
-        while step < n_narrow:
-            sums = call(add_kernel, small, 2, name="sectors")(sums, exchange(sums, "narrow", step))
-            step *= 2
+    for step in ([3] if n_narrow >= 4 else []) + [1] + [1 << bit for bit in range(2, n_narrow.bit_length() - 1)]:
+        if others:
+            sums = call(add_kernel, small, 2, name="sectors")(sums, *others)
+        others = [exchange(sums, "narrow", step)]
 
     out, alpha = call(
         functools.partial(final_kernel, len(parts)), [f32(band, block), f32(1, 128)], 2 + len(parts) + len(others),

time: 43.5 us -> 43.9 us (level)
  the two profiles are of different devices: /device:TPU:6 before, /device:TPU:0 now
where the time goes in v1:
time: 43.9 us; the launch traced here: 43.8 us
  starting transfers between devices  19.7 us (45%)
  waiting for transfers between devices  11.5 us (26%)
  Pallas kernels  10.6 us (24%)
  local copies, waits for them, and re-layouts  1.28 us (3%)
  between operations  0.76 us (2%)
    ppermute x8, starting transfers between devices, exchange(): return lax.ppermute(value, axis, [(i, i ^ shift) for i in range(count)])  18.3 us
    ppermute x8, waiting for transfers between devices, exchange(): return lax.ppermute(value, axis, [(i, i ^ shift) for i in range(count)])  11.5 us
    pallas_call x1, Pallas kernels, per_device(): pl.pallas_call(main_kernel, out_shape=[jax.ShapeDtypeStruct((8, 128), jnp...  8.85 us
    ppermute x2, starting transfers between devices, per_device(): lax.ppermute(rows, 'narrow', across + ends)  1.39 us
    slice x1, local copies, waits for them, and re-layouts, per_device(): own[:half]  1.27 us
  transfers between devices with their start and end apart: 10, of which 5 were waited for; matrix products, arithmetic and copies ran while one was open for 3% of the time, Pallas kernels for 21%

profile of v1, /device:TPU:0, one launch (start us, length us, event | category | flops | bytes accessed | tf_op | source)
XLA Modules:
  0.0 43.8 jit_solution(12934188094439473541)
XLA Ops:
  0.6 0.0 copy-start.2
  0.6 0.0 copy-start.1
  0.7 0.0 copy-start
  0.7 0.5 %collective-permute-start = (f32[512,512]{1,0:T(8,128)}, f32[512,512]{1,0:T(8,128)S(1)}, u32[]{:S(2)}, u32[]{:S(2)}) collective-permute-start(f32[512,512]{1,0:T(8,128)} %bitcast.8), channel_id=1, source_target_pairs={{0,1},{1,0},{2,3},{3,2},{4,5},{5,4},{6,7},{7,6},{8,9},{9,8},{10,11... | collective-permute-start | bytes 3145736 | tf_op jit(solution)/shard_map/ppermute | solution.py:257
  1.2 1.3 %slice_bitcast_fusion = (f32[256,512]{1,0:T(8,128)S(1)}, f32[256,512]{1,0:T(8,128)S(1)}) fusion(f32[1,512,512]{2,1,0:T(8,128)} %state.1), kind=kLoop, calls=%fused_computation | loop fusion | bytes 2097152 | tf_op jit(solution)/shard_map/slice | solution.py:291
  2.4 0.7 %collective-permute-start.2 = (f32[256,512]{1,0:T(8,128)S(1)}, f32[256,512]{1,0:T(8,128)S(1)}, u32[]{:S(2)}, u32[]{:S(2)}) collective-permute-start(f32[256,512]{1,0:T(8,128)S(1)} %get-tuple-element.38), channel_id=1, source_target_pairs={{1,2},{2,1},{0,0},{3,3},{5,6},{6,5},{4,4},{7,7},{9,10},{10,9},{8,8... | collective-permute-start | bytes 1572872 | tf_op jit(solution)/shard_map/ppermute | solution.py:291
  3.2 0.7 %collective-permute-start.1 = (f32[256,512]{1,0:T(8,128)S(1)}, f32[256,512]{1,0:T(8,128)S(1)}, u32[]{:S(2)}, u32[]{:S(2)}) collective-permute-start(f32[256,512]{1,0:T(8,128)S(1)} %get-tuple-element.39), channel_id=1, source_target_pairs={{1,2},{2,1},{0,0},{3,3},{5,6},{6,5},{4,4},{7,7},{9,10},{10,9},{8,8... | collective-permute-start | bytes 1572872 | tf_op jit(solution)/shard_map/ppermute | solution.py:291
  3.9 0.0 collective-permute-done.near
  3.9 0.0 copy-done.2
  3.9 0.0 copy-done.1
  3.9 0.0 copy-done
  3.9 8.9 %main.1 = (s32[8,128]{1,0:T(8,128)S(1)}, f32[512,512]{1,0:T(8,128)S(1)}, f32[64,512]{1,0:T(8,128)S(1)}, f32[8,128]{1,0:T(8,128)S(1)}, bf16[4,512,512]{2,1,0:T(8,...) custom-call(s32[4]{0:T(128)S(1)} %copy-done, ...), custom_call_target="tpu_custom_call" | custom-call | flops 3221225472 | bytes 8388608 | tf_op jit(solution)/shard_map/main/pallas_call | solution.py:295
  12.8 0.0 collective-permute-done.2.far
  12.8 0.3 far.1.before
  13.1 0.0 collective-permute-done.1.far
  13.1 0.7 %last.1 = (f32[136,512]{1,0:T(8,128)S(1)}, f32[136,512]{1,0:T(8,128)S(1)}, f32[136,512]{1,0:T(8,128)S(1)}, f32[136,512]{1,0:T(8,128)S(1)}) custom-call(s32[8,128]{1,0:T(8,128)S(1)} %get-tuple-element.21.table, f32[256,512]{1,0:T(8,128)S(1)} %collective-permute-done.1.far, bf16[4,512,512]{2,1,0:T(8,128)(2,1)S(1)} %get-tuple-element.22.lh, ...), custom_call_target="tpu_custom_call" | custom-call | flops 3221225472 | bytes 1048576 | tf_op jit(solution)/shard_map/last/pallas_call | solution.py:329
  13.8 2.2 %collective-permute-start.3 = (f32[136,512]{1,0:T(8,128)S(1)}, f32[136,512]{1,0:T(8,128)S(1)}, u32[]{:S(2)}, u32[]{:S(2)}) collective-permute-start(f32[136,512]{1,0:T(8,128)S(1)} %get-tuple-element.30), channel_id=1, source_target_pairs={{0,12},{4,8},{8,4},{12,0},{16,28},{20,24},{24,20},{28,16},{1,13},{... | collective-permute-start | bytes 835592 | tf_op jit(solution)/shard_map/ppermute | solution.py:257
  16.0 2.3 %collective-permute-start.4 = (f32[136,512]{1,0:T(8,128)S(1)}, f32[136,512]{1,0:T(8,128)S(1)}, u32[]{:S(2)}, u32[]{:S(2)}) collective-permute-start(f32[136,512]{1,0:T(8,128)S(1)} %get-tuple-element.31), channel_id=1, source_target_pairs={{0,8},{4,12},{8,0},{12,4},{16,24},{20,28},{24,16},{28,20},{1,9},{5... | collective-permute-start | bytes 835592 | tf_op jit(solution)/shard_map/ppermute | solution.py:257
  18.2 1.4 %collective-permute-start.5 = (f32[136,512]{1,0:T(8,128)S(1)}, f32[136,512]{1,0:T(8,128)S(1)}, u32[]{:S(2)}, u32[]{:S(2)}) collective-permute-start(f32[136,512]{1,0:T(8,128)S(1)} %get-tuple-element.32), channel_id=1, source_target_pairs={{0,4},{4,0},{8,12},{12,8},{16,20},{20,16},{24,28},{28,24},{1,5},{5... | collective-permute-start | bytes 835592 | tf_op jit(solution)/shard_map/ppermute | solution.py:257
  19.6 1.7 %collective-permute-done.3.refs_1_ = f32[136,512]{1,0:T(8,128)S(1)} collective-permute-done((f32[136,512]{1,0:T(8,128)S(1)}, f32[136,512]{1,0:T(8,128)S(1)}, u32[]{:S(2)}, u32[]{:S(2)}) %collective-permute-start.3) | collective-permute-done | bytes 278560 | tf_op jit(solution)/shard_map/ppermute | solution.py:257
  21.3 4.4 %collective-permute-done.4.refs_2_ = f32[136,512]{1,0:T(8,128)S(1)} collective-permute-done((f32[136,512]{1,0:T(8,128)S(1)}, f32[136,512]{1,0:T(8,128)S(1)}, u32[]{:S(2)}, u32[]{:S(2)}) %collective-permute-start.4) | collective-permute-done | bytes 278560 | tf_op jit(solution)/shard_map/ppermute | solution.py:257
  25.7 0.0 collective-permute-done.5.refs_3_
  25.7 0.1 merge.1
  25.8 4.0 %collective-permute-start.7 = (f32[8,128]{1,0:T(8,128)S(1)}, f32[8,128]{1,0:T(8,128)S(1)}, u32[]{:S(2)}, u32[]{:S(2)}) collective-permute-start(f32[8,128]{1,0:T(8,128)S(1)} %get-tuple-element.35.refs_0_), channel_id=1, source_target_pairs={{0,16},{4,20},{8,24},{12,28},{16,0},{20,4},{24,8},{28,12},{1,17},{... | collective-permute-start | bytes 12296 | tf_op jit(solution)/shard_map/ppermute | solution.py:257
  29.7 0.1 collective-permute-start.6
  29.8 1.6 %collective-permute-done.7.refs_1_ = f32[8,128]{1,0:T(8,128)S(1)} collective-permute-done((f32[8,128]{1,0:T(8,128)S(1)}, f32[8,128]{1,0:T(8,128)S(1)}, u32[]{:S(2)}, u32[]{:S(2)}) %collective-permute-start.7) | collective-permute-done | bytes 4128 | tf_op jit(solution)/shard_map/ppermute | solution.py:257
  31.4 0.0 collective-permute-start.8
  31.4 3.0 %collective-permute-done.8.refs_1_ = f32[8,128]{1,0:T(8,128)S(1)} collective-permute-done((f32[8,128]{1,0:T(8,128)S(1)}, f32[8,128]{1,0:T(8,128)S(1)}, u32[]{:S(2)}, u32[]{:S(2)}) %collective-permute-start.8) | collective-permute-done | bytes 4128 | tf_op jit(solution)/shard_map/ppermute | solution.py:257
  34.5 7.9 %collective-permute-start.9 = (f32[8,128]{1,0:T(8,128)S(1)}, f32[8,128]{1,0:T(8,128)S(1)}, u32[]{:S(2)}, u32[]{:S(2)}) collective-permute-start(f32[8,128]{1,0:T(8,128)S(1)} %sectors.1.rest_2_), channel_id=1, source_target_pairs={{0,1},{1,0},{2,3},{3,2},{4,5},{5,4},{6,7},{7,6},{8,9},{9,8},{10,11... | collective-permute-start | bytes 12296 | tf_op jit(solution)/shard_map/ppermute | solution.py:257
  42.3 0.8 %collective-permute-done.9.rest_3_ = f32[8,128]{1,0:T(8,128)S(1)} collective-permute-done((f32[8,128]{1,0:T(8,128)S(1)}, f32[8,128]{1,0:T(8,128)S(1)}, u32[]{:S(2)}, u32[]{:S(2)}) %collective-permute-start.9) | collective-permute-done | bytes 4128 | tf_op jit(solution)/shard_map/ppermute | solution.py:257
  43.2 0.0 collective-permute-done.6.rest_1_
  43.2 0.7 %final.1 = (f32[64,512]{1,0:T(8,128)}, f32[1,128]{1,0:T(1,128)}) custom-call(f32[64,512]{1,0:T(8,128)S(1)} %get-tuple-element.20.psi, f32[64,512]{1,0:T(8,128)S(1)} %get-tuple-element.33.rest_0_, f32[64,512]{1,0:T(8,128)S(1)} %collective-permute-done.6.rest_1_, f32[8,128]{1,0:T(8,128)S(1)} %sectors.1.rest_2_, f32[8,128]{1,0:T(8,128)S(1)} %collective-permute-done.9.rest_3_), custom_call_target="tpu_custom_call" | custom-call | tf_op jit(solution)/shard_map/final/pallas_call | solution.py:352
  (2 shorter events, 0.0 us)
Async XLA Ops:
  0.6 3.2 %copy-start.2 = (s32[4]{0:T(128)S(1)}, s32[4]{0:T(128)}, u32[]{:S(2)}) copy-start(s32[4]{0:T(128)} %charge.1) | copy-start | bytes 52
  0.6 3.2 %copy-start.1 = (s32[4]{0:T(128)S(1)}, s32[4]{0:T(128)}, u32[]{:S(2)}) copy-start(s32[4]{0:T(128)} %rsz.1) | copy-start | bytes 52
  0.7 3.2 %copy-start = (s32[4]{0:T(128)S(1)}, s32[4]{0:T(128)}, u32[]{:S(2)}) copy-start(s32[4]{0:T(128)} %lsz.1) | copy-start | bytes 52
  0.7 3.2 %collective-permute-start = (f32[512,512]{1,0:T(8,128)}, f32[512,512]{1,0:T(8,128)S(1)}, u32[]{:S(2)}, u32[]{:S(2)}) collective-permute-start(f32[512,512]{1,0:T(8,128)} %bitcast.8), channel_id=1, source_target_pairs={{0,1},{1,0},{2,3},{3,2},{4,5},{5,4},{6,7},{7,6},{8,9},{9,8},{10,11... | collective-permute-start | bytes 3145736 | tf_op jit(solution)/shard_map/ppermute | solution.py:257
  2.4 10.3 %collective-permute-start.2 = (f32[256,512]{1,0:T(8,128)S(1)}, f32[256,512]{1,0:T(8,128)S(1)}, u32[]{:S(2)}, u32[]{:S(2)}) collective-permute-start(f32[256,512]{1,0:T(8,128)S(1)} %get-tuple-element.38), channel_id=1, source_target_pairs={{1,2},{2,1},{0,0},{3,3},{5,6},{6,5},{4,4},{7,7},{9,10},{10,9},{8,8... | collective-permute-start | bytes 1572872 | tf_op jit(solution)/shard_map/ppermute | solution.py:291
  3.2 10.0 %collective-permute-start.1 = (f32[256,512]{1,0:T(8,128)S(1)}, f32[256,512]{1,0:T(8,128)S(1)}, u32[]{:S(2)}, u32[]{:S(2)}) collective-permute-start(f32[256,512]{1,0:T(8,128)S(1)} %get-tuple-element.39), channel_id=1, source_target_pairs={{1,2},{2,1},{0,0},{3,3},{5,6},{6,5},{4,4},{7,7},{9,10},{10,9},{8,8... | collective-permute-start | bytes 1572872 | tf_op jit(solution)/shard_map/ppermute | solution.py:291
  13.8 7.5 %collective-permute-start.3 = (f32[136,512]{1,0:T(8,128)S(1)}, f32[136,512]{1,0:T(8,128)S(1)}, u32[]{:S(2)}, u32[]{:S(2)}) collective-permute-start(f32[136,512]{1,0:T(8,128)S(1)} %get-tuple-element.30), channel_id=1, source_target_pairs={{0,12},{4,8},{8,4},{12,0},{16,28},{20,24},{24,20},{28,16},{1,13},{... | collective-permute-start | bytes 835592 | tf_op jit(solution)/shard_map/ppermute | solution.py:257
  16.0 9.7 %collective-permute-start.4 = (f32[136,512]{1,0:T(8,128)S(1)}, f32[136,512]{1,0:T(8,128)S(1)}, u32[]{:S(2)}, u32[]{:S(2)}) collective-permute-start(f32[136,512]{1,0:T(8,128)S(1)} %get-tuple-element.31), channel_id=1, source_target_pairs={{0,8},{4,12},{8,0},{12,4},{16,24},{20,28},{24,16},{28,20},{1,9},{5... | collective-permute-start | bytes 835592 | tf_op jit(solution)/shard_map/ppermute | solution.py:257
  18.2 7.4 %collective-permute-start.5 = (f32[136,512]{1,0:T(8,128)S(1)}, f32[136,512]{1,0:T(8,128)S(1)}, u32[]{:S(2)}, u32[]{:S(2)}) collective-permute-start(f32[136,512]{1,0:T(8,128)S(1)} %get-tuple-element.32), channel_id=1, source_target_pairs={{0,4},{4,0},{8,12},{12,8},{16,20},{20,16},{24,28},{28,24},{1,5},{5... | collective-permute-start | bytes 835592 | tf_op jit(solution)/shard_map/ppermute | solution.py:257
  25.8 5.7 %collective-permute-start.7 = (f32[8,128]{1,0:T(8,128)S(1)}, f32[8,128]{1,0:T(8,128)S(1)}, u32[]{:S(2)}, u32[]{:S(2)}) collective-permute-start(f32[8,128]{1,0:T(8,128)S(1)} %get-tuple-element.35.refs_0_), channel_id=1, source_target_pairs={{0,16},{4,20},{8,24},{12,28},{16,0},{20,4},{24,8},{28,12},{1,17},{... | collective-permute-start | bytes 12296 | tf_op jit(solution)/shard_map/ppermute | solution.py:257
  29.7 13.4 %collective-permute-start.6 = (f32[64,512]{1,0:T(8,128)S(1)}, f32[64,512]{1,0:T(8,128)S(1)}, u32[]{:S(2)}, u32[]{:S(2)}) collective-permute-start(f32[64,512]{1,0:T(8,128)S(1)} %get-tuple-element.34), channel_id=1, source_target_pairs={{0,16},{4,20},{8,24},{12,28},{16,0},{20,4},{24,8},{28,12},{1,17},{... | collective-permute-start | bytes 393224 | tf_op jit(solution)/shard_map/ppermute | solution.py:257
  31.4 3.0 %collective-permute-start.8 = (f32[8,128]{1,0:T(8,128)S(1)}, f32[8,128]{1,0:T(8,128)S(1)}, u32[]{:S(2)}, u32[]{:S(2)}) collective-permute-start(f32[8,128]{1,0:T(8,128)S(1)} %wide.1.refs_0_), channel_id=1, source_target_pairs={{0,3},{1,2},{2,1},{3,0},{4,7},{5,6},{6,5},{7,4},{8,11},{9,10},{10,... | collective-permute-start | bytes 12296 | tf_op jit(solution)/shard_map/ppermute | solution.py:257
  34.5 8.7 %collective-permute-start.9 = (f32[8,128]{1,0:T(8,128)S(1)}, f32[8,128]{1,0:T(8,128)S(1)}, u32[]{:S(2)}, u32[]{:S(2)}) collective-permute-start(f32[8,128]{1,0:T(8,128)S(1)} %sectors.1.rest_2_), channel_id=1, source_target_pairs={{0,1},{1,0},{2,3},{3,2},{4,5},{5,4},{6,7},{7,6},{8,9},{9,8},{10,11... | collective-permute-start | bytes 12296 | tf_op jit(solution)/shard_map/ppermute | solution.py:257

commit v2 on v1

--- a/solution.py
+++ b/solution.py
@@ -286,9 +286,8 @@
     square, small = f32(block, block), f32(8, 128)
     work = 6 * chans * block**3
 
-    ends = [(0, 0), (n_narrow - 1, n_narrow - 1)]
     across = [pair for k in range(1, n_narrow - 1, 2) for pair in ((k, k + 1), (k + 1, k))]
-    far_top, far_low = (lax.ppermute(rows, "narrow", across + ends) for rows in (own[:half], own[half:]))
+    far_top, far_low = (lax.ppermute(rows, "narrow", across) for rows in (own[:half], own[half:]))
     near = exchange(own, "narrow", 1)
 
     halves = jax.ShapeDtypeStruct((chans, block, block), BF16)

time: 43.9 us -> 43.5 us (level)
  Pallas kernels: 10.6 us -> 9.08 us
  waiting for transfers between devices: 11.5 us -> 12.9 us
  starting transfers between devices: 19.7 us -> 19 us
    pallas_call x1, Pallas kernels: 8.85 us -> 7.3 us  [per_device(): pl.pallas_call(main_kernel, out_shape=[jax.ShapeDtypeStruct((8, 128), jnp...]
    ppermute x8, waiting for transfers between devices: 11.5 us -> 12.9 us  [exchange(): return lax.ppermute(value, axis, [(i, i ^ shift) for i in range(count)])]
    ppermute x8, starting transfers between devices: 18.3 us -> 17.6 us  [exchange(): return lax.ppermute(value, axis, [(i, i ^ shift) for i in range(count)])]
  transfers between devices with their start and end apart: 10 -> 10, of which waited for: 5 -> 5; matrix products, arithmetic and copies ran while one was open for 3% -> 3% of each run, Pallas kernels for 21% -> 18%
where the time goes in v2:
time: 43.5 us; the launch traced here: 43 us
  starting transfers between devices  19 us (44%)
  waiting for transfers between devices  12.9 us (30%)
  Pallas kernels  9.08 us (21%)
  local copies, waits for them, and re-layouts  1.28 us (3%)
  between operations  0.76 us (2%)
    ppermute x8, starting transfers between devices, exchange(): return lax.ppermute(value, axis, [(i, i ^ shift) for i in range(count)])  17.6 us
    ppermute x8, waiting for transfers between devices, exchange(): return lax.ppermute(value, axis, [(i, i ^ shift) for i in range(count)])  12.9 us
    pallas_call x1, Pallas kernels, per_device(): pl.pallas_call(main_kernel, out_shape=[jax.ShapeDtypeStruct((8, 128), jnp...  7.3 us
    ppermute x2, starting transfers between devices, per_device(): lax.ppermute(rows, 'narrow', across)  1.39 us
    slice x1, local copies, waits for them, and re-layouts, per_device(): own[:half]  1.27 us
  transfers between devices with their start and end apart: 10, of which 5 were waited for; matrix products, arithmetic and copies ran while one was open for 3% of the time, Pallas kernels for 18%

profile of v2, /device:TPU:0, one launch (start us, length us, event | category | flops | bytes accessed | tf_op | source)
XLA Modules:
  0.0 43.0 jit_solution(6523570900941621202)
XLA Ops:
  0.6 0.0 copy-start.2
  0.6 0.0 copy-start.1
  0.7 0.0 copy-start
  0.7 0.5 %collective-permute-start = (f32[512,512]{1,0:T(8,128)}, f32[512,512]{1,0:T(8,128)S(1)}, u32[]{:S(2)}, u32[]{:S(2)}) collective-permute-start(f32[512,512]{1,0:T(8,128)} %bitcast.8), channel_id=1, source_target_pairs={{0,1},{1,0},{2,3},{3,2},{4,5},{5,4},{6,7},{7,6},{8,9},{9,8},{10,11... | collective-permute-start | bytes 3145736 | tf_op jit(solution)/shard_map/ppermute | solution.py:257
  1.2 1.3 %slice_bitcast_fusion = (f32[256,512]{1,0:T(8,128)S(1)}, f32[256,512]{1,0:T(8,128)S(1)}) fusion(f32[1,512,512]{2,1,0:T(8,128)} %state.1), kind=kLoop, calls=%fused_computation | loop fusion | bytes 2097152 | tf_op jit(solution)/shard_map/slice | solution.py:290
  2.4 0.7 %collective-permute-start.2 = (f32[256,512]{1,0:T(8,128)S(1)}, f32[256,512]{1,0:T(8,128)S(1)}, u32[]{:S(2)}, u32[]{:S(2)}) collective-permute-start(f32[256,512]{1,0:T(8,128)S(1)} %get-tuple-element.38), channel_id=1, source_target_pairs={{1,2},{2,1},{5,6},{6,5},{9,10},{10,9},{13,14},{14,13},{17,18},{18,... | collective-permute-start | bytes 1572872 | tf_op jit(solution)/shard_map/ppermute | solution.py:290
  3.2 0.7 %collective-permute-start.1 = (f32[256,512]{1,0:T(8,128)S(1)}, f32[256,512]{1,0:T(8,128)S(1)}, u32[]{:S(2)}, u32[]{:S(2)}) collective-permute-start(f32[256,512]{1,0:T(8,128)S(1)} %get-tuple-element.39), channel_id=1, source_target_pairs={{1,2},{2,1},{5,6},{6,5},{9,10},{10,9},{13,14},{14,13},{17,18},{18,... | collective-permute-start | bytes 1572872 | tf_op jit(solution)/shard_map/ppermute | solution.py:290
  3.9 0.0 collective-permute-done.near
  3.9 0.0 copy-done.2
  3.9 0.0 copy-done.1
  3.9 0.0 copy-done
  3.9 7.3 %main.1 = (s32[8,128]{1,0:T(8,128)S(1)}, f32[512,512]{1,0:T(8,128)S(1)}, f32[64,512]{1,0:T(8,128)S(1)}, f32[8,128]{1,0:T(8,128)S(1)}, bf16[4,512,512]{2,1,0:T(8,...) custom-call(s32[4]{0:T(128)S(1)} %copy-done, ...), custom_call_target="tpu_custom_call" | custom-call | flops 3221225472 | bytes 8388608 | tf_op jit(solution)/shard_map/main/pallas_call | solution.py:294
  11.2 0.0 collective-permute-done.2.far
  11.2 0.3 far.1.before
  11.6 0.0 collective-permute-done.1.far
  11.6 0.7 %last.1 = (f32[136,512]{1,0:T(8,128)S(1)}, f32[136,512]{1,0:T(8,128)S(1)}, f32[136,512]{1,0:T(8,128)S(1)}, f32[136,512]{1,0:T(8,128)S(1)}) custom-call(s32[8,128]{1,0:T(8,128)S(1)} %get-tuple-element.21.table, f32[256,512]{1,0:T(8,128)S(1)} %collective-permute-done.1.far, bf16[4,512,512]{2,1,0:T(8,128)(2,1)S(1)} %get-tuple-element.22.lh, ...), custom_call_target="tpu_custom_call" | custom-call | flops 3221225472 | bytes 1048576 | tf_op jit(solution)/shard_map/last/pallas_call | solution.py:328
  12.2 3.7 %collective-permute-start.3 = (f32[136,512]{1,0:T(8,128)S(1)}, f32[136,512]{1,0:T(8,128)S(1)}, u32[]{:S(2)}, u32[]{:S(2)}) collective-permute-start(f32[136,512]{1,0:T(8,128)S(1)} %get-tuple-element.30), channel_id=1, source_target_pairs={{0,12},{4,8},{8,4},{12,0},{16,28},{20,24},{24,20},{28,16},{1,13},{... | collective-permute-start | bytes 835592 | tf_op jit(solution)/shard_map/ppermute | solution.py:257
  16.0 2.0 %collective-permute-start.4 = (f32[136,512]{1,0:T(8,128)S(1)}, f32[136,512]{1,0:T(8,128)S(1)}, u32[]{:S(2)}, u32[]{:S(2)}) collective-permute-start(f32[136,512]{1,0:T(8,128)S(1)} %get-tuple-element.31), channel_id=1, source_target_pairs={{0,8},{4,12},{8,0},{12,4},{16,24},{20,28},{24,16},{28,20},{1,9},{5... | collective-permute-start | bytes 835592 | tf_op jit(solution)/shard_map/ppermute | solution.py:257
  18.0 0.1 collective-permute-start.5
  18.1 2.4 %collective-permute-done.3.refs_1_ = f32[136,512]{1,0:T(8,128)S(1)} collective-permute-done((f32[136,512]{1,0:T(8,128)S(1)}, f32[136,512]{1,0:T(8,128)S(1)}, u32[]{:S(2)}, u32[]{:S(2)}) %collective-permute-start.3) | collective-permute-done | bytes 278560 | tf_op jit(solution)/shard_map/ppermute | solution.py:257
  20.5 5.0 %collective-permute-done.4.refs_2_ = f32[136,512]{1,0:T(8,128)S(1)} collective-permute-done((f32[136,512]{1,0:T(8,128)S(1)}, f32[136,512]{1,0:T(8,128)S(1)}, u32[]{:S(2)}, u32[]{:S(2)}) %collective-permute-start.4) | collective-permute-done | bytes 278560 | tf_op jit(solution)/shard_map/ppermute | solution.py:257
  25.5 0.0 collective-permute-done.5.refs_3_
  25.5 0.1 merge.1
  25.6 4.7 %collective-permute-start.7 = (f32[8,128]{1,0:T(8,128)S(1)}, f32[8,128]{1,0:T(8,128)S(1)}, u32[]{:S(2)}, u32[]{:S(2)}) collective-permute-start(f32[8,128]{1,0:T(8,128)S(1)} %get-tuple-element.35.refs_0_), channel_id=1, source_target_pairs={{0,16},{4,20},{8,24},{12,28},{16,0},{20,4},{24,8},{28,12},{1,17},{... | collective-permute-start | bytes 12296 | tf_op jit(solution)/shard_map/ppermute | solution.py:257
  30.3 0.1 collective-permute-start.6
  30.4 1.6 %collective-permute-done.7.refs_1_ = f32[8,128]{1,0:T(8,128)S(1)} collective-permute-done((f32[8,128]{1,0:T(8,128)S(1)}, f32[8,128]{1,0:T(8,128)S(1)}, u32[]{:S(2)}, u32[]{:S(2)}) %collective-permute-start.7) | collective-permute-done | bytes 4128 | tf_op jit(solution)/shard_map/ppermute | solution.py:257
  32.0 0.0 collective-permute-start.8
  32.0 3.0 %collective-permute-done.8.refs_1_ = f32[8,128]{1,0:T(8,128)S(1)} collective-permute-done((f32[8,128]{1,0:T(8,128)S(1)}, f32[8,128]{1,0:T(8,128)S(1)}, u32[]{:S(2)}, u32[]{:S(2)}) %collective-permute-start.8) | collective-permute-done | bytes 4128 | tf_op jit(solution)/shard_map/ppermute | solution.py:257
  35.1 6.5 %collective-permute-start.9 = (f32[8,128]{1,0:T(8,128)S(1)}, f32[8,128]{1,0:T(8,128)S(1)}, u32[]{:S(2)}, u32[]{:S(2)}) collective-permute-start(f32[8,128]{1,0:T(8,128)S(1)} %sectors.1.rest_2_), channel_id=1, source_target_pairs={{0,1},{1,0},{2,3},{3,2},{4,5},{5,4},{6,7},{7,6},{8,9},{9,8},{10,11... | collective-permute-start | bytes 12296 | tf_op jit(solution)/shard_map/ppermute | solution.py:257
  41.5 0.8 %collective-permute-done.9.rest_3_ = f32[8,128]{1,0:T(8,128)S(1)} collective-permute-done((f32[8,128]{1,0:T(8,128)S(1)}, f32[8,128]{1,0:T(8,128)S(1)}, u32[]{:S(2)}, u32[]{:S(2)}) %collective-permute-start.9) | collective-permute-done | bytes 4128 | tf_op jit(solution)/shard_map/ppermute | solution.py:257
  42.4 0.0 collective-permute-done.6.rest_1_
  42.4 0.7 %final.1 = (f32[64,512]{1,0:T(8,128)}, f32[1,128]{1,0:T(1,128)}) custom-call(f32[64,512]{1,0:T(8,128)S(1)} %get-tuple-element.20.psi, f32[64,512]{1,0:T(8,128)S(1)} %get-tuple-element.33.rest_0_, f32[64,512]{1,0:T(8,128)S(1)} %collective-permute-done.6.rest_1_, f32[8,128]{1,0:T(8,128)S(1)} %sectors.1.rest_2_, f32[8,128]{1,0:T(8,128)S(1)} %collective-permute-done.9.rest_3_), custom_call_target="tpu_custom_call" | custom-call | tf_op jit(solution)/shard_map/final/pallas_call | solution.py:351
  (2 shorter events, 0.0 us)
Async XLA Ops:
  0.6 3.2 %copy-start.2 = (s32[4]{0:T(128)S(1)}, s32[4]{0:T(128)}, u32[]{:S(2)}) copy-start(s32[4]{0:T(128)} %charge.1) | copy-start | bytes 52
  0.6 3.2 %copy-start.1 = (s32[4]{0:T(128)S(1)}, s32[4]{0:T(128)}, u32[]{:S(2)}) copy-start(s32[4]{0:T(128)} %rsz.1) | copy-start | bytes 52
  0.7 3.2 %copy-start = (s32[4]{0:T(128)S(1)}, s32[4]{0:T(128)}, u32[]{:S(2)}) copy-start(s32[4]{0:T(128)} %lsz.1) | copy-start | bytes 52
  0.7 3.2 %collective-permute-start = (f32[512,512]{1,0:T(8,128)}, f32[512,512]{1,0:T(8,128)S(1)}, u32[]{:S(2)}, u32[]{:S(2)}) collective-permute-start(f32[512,512]{1,0:T(8,128)} %bitcast.8), channel_id=1, source_target_pairs={{0,1},{1,0},{2,3},{3,2},{4,5},{5,4},{6,7},{7,6},{8,9},{9,8},{10,11... | collective-permute-start | bytes 3145736 | tf_op jit(solution)/shard_map/ppermute | solution.py:257
  2.4 8.8 %collective-permute-start.2 = (f32[256,512]{1,0:T(8,128)S(1)}, f32[256,512]{1,0:T(8,128)S(1)}, u32[]{:S(2)}, u32[]{:S(2)}) collective-permute-start(f32[256,512]{1,0:T(8,128)S(1)} %get-tuple-element.38), channel_id=1, source_target_pairs={{1,2},{2,1},{5,6},{6,5},{9,10},{10,9},{13,14},{14,13},{17,18},{18,... | collective-permute-start | bytes 1572872 | tf_op jit(solution)/shard_map/ppermute | solution.py:290
  3.2 8.4 %collective-permute-start.1 = (f32[256,512]{1,0:T(8,128)S(1)}, f32[256,512]{1,0:T(8,128)S(1)}, u32[]{:S(2)}, u32[]{:S(2)}) collective-permute-start(f32[256,512]{1,0:T(8,128)S(1)} %get-tuple-element.39), channel_id=1, source_target_pairs={{1,2},{2,1},{5,6},{6,5},{9,10},{10,9},{13,14},{14,13},{17,18},{18,... | collective-permute-start | bytes 1572872 | tf_op jit(solution)/shard_map/ppermute | solution.py:290
  12.2 8.3 %collective-permute-start.3 = (f32[136,512]{1,0:T(8,128)S(1)}, f32[136,512]{1,0:T(8,128)S(1)}, u32[]{:S(2)}, u32[]{:S(2)}) collective-permute-start(f32[136,512]{1,0:T(8,128)S(1)} %get-tuple-element.30), channel_id=1, source_target_pairs={{0,12},{4,8},{8,4},{12,0},{16,28},{20,24},{24,20},{28,16},{1,13},{... | collective-permute-start | bytes 835592 | tf_op jit(solution)/shard_map/ppermute | solution.py:257
  16.0 9.5 %collective-permute-start.4 = (f32[136,512]{1,0:T(8,128)S(1)}, f32[136,512]{1,0:T(8,128)S(1)}, u32[]{:S(2)}, u32[]{:S(2)}) collective-permute-start(f32[136,512]{1,0:T(8,128)S(1)} %get-tuple-element.31), channel_id=1, source_target_pairs={{0,8},{4,12},{8,0},{12,4},{16,24},{20,28},{24,16},{28,20},{1,9},{5... | collective-permute-start | bytes 835592 | tf_op jit(solution)/shard_map/ppermute | solution.py:257
  18.0 7.6 %collective-permute-start.5 = (f32[136,512]{1,0:T(8,128)S(1)}, f32[136,512]{1,0:T(8,128)S(1)}, u32[]{:S(2)}, u32[]{:S(2)}) collective-permute-start(f32[136,512]{1,0:T(8,128)S(1)} %get-tuple-element.32), channel_id=1, source_target_pairs={{0,4},{4,0},{8,12},{12,8},{16,20},{20,16},{24,28},{28,24},{1,5},{5... | collective-permute-start | bytes 835592 | tf_op jit(solution)/shard_map/ppermute | solution.py:257
  25.6 6.4 %collective-permute-start.7 = (f32[8,128]{1,0:T(8,128)S(1)}, f32[8,128]{1,0:T(8,128)S(1)}, u32[]{:S(2)}, u32[]{:S(2)}) collective-permute-start(f32[8,128]{1,0:T(8,128)S(1)} %get-tuple-element.35.refs_0_), channel_id=1, source_target_pairs={{0,16},{4,20},{8,24},{12,28},{16,0},{20,4},{24,8},{28,12},{1,17},{... | collective-permute-start | bytes 12296 | tf_op jit(solution)/shard_map/ppermute | solution.py:257
  30.3 12.0 %collective-permute-start.6 = (f32[64,512]{1,0:T(8,128)S(1)}, f32[64,512]{1,0:T(8,128)S(1)}, u32[]{:S(2)}, u32[]{:S(2)}) collective-permute-start(f32[64,512]{1,0:T(8,128)S(1)} %get-tuple-element.34), channel_id=1, source_target_pairs={{0,16},{4,20},{8,24},{12,28},{16,0},{20,4},{24,8},{28,12},{1,17},{... | collective-permute-start | bytes 393224 | tf_op jit(solution)/shard_map/ppermute | solution.py:257
  32.0 3.0 %collective-permute-start.8 = (f32[8,128]{1,0:T(8,128)S(1)}, f32[8,128]{1,0:T(8,128)S(1)}, u32[]{:S(2)}, u32[]{:S(2)}) collective-permute-start(f32[8,128]{1,0:T(8,128)S(1)} %wide.1.refs_0_), channel_id=1, source_target_pairs={{0,3},{1,2},{2,1},{3,0},{4,7},{5,6},{6,5},{7,4},{8,11},{9,10},{10,... | collective-permute-start | bytes 12296 | tf_op jit(solution)/shard_map/ppermute | solution.py:257
  35.1 7.3 %collective-permute-start.9 = (f32[8,128]{1,0:T(8,128)S(1)}, f32[8,128]{1,0:T(8,128)S(1)}, u32[]{:S(2)}, u32[]{:S(2)}) collective-permute-start(f32[8,128]{1,0:T(8,128)S(1)} %sectors.1.rest_2_), channel_id=1, source_target_pairs={{0,1},{1,0},{2,3},{3,2},{4,5},{5,4},{6,7},{7,6},{8,9},{9,8},{10,11... | collective-permute-start | bytes 12296 | tf_op jit(solution)/shard_map/ppermute | solution.py:257

commit v3 on v1

--- a/solution.py
+++ b/solution.py
@@ -344,7 +344,7 @@
         mine, give = call(halves_kernel, [f32(held * band, block)] * 2, 2, name="halves")(*parts)
         parts = [mine, exchange(give, "wide", groups * held)]
     others = []
-    for step in ([3] if n_narrow >= 4 else []) + [1] + [1 << bit for bit in range(2, n_narrow.bit_length() - 1)]:
+    for step in [1] + ([3] if n_narrow >= 4 else []) + [1 << bit for bit in range(2, n_narrow.bit_length() - 1)]:
         if others:
             sums = call(add_kernel, small, 2, name="sectors")(sums, *others)
         others = [exchange(sums, "narrow", step)]

time: 43.9 us -> 44.2 us (level); the launches traced: 43.8 us -> 43.4 us
  waiting for transfers between devices: 11.5 us -> 11 us
    ppermute x8, waiting for transfers between devices: 11.5 us -> 11 us  [exchange(): return lax.ppermute(value, axis, [(i, i ^ shift) for i in range(count)])]
  transfers between devices with their start and end apart: 10 -> 10, of which waited for: 5 -> 6; matrix products, arithmetic and copies ran while one was open for 3% -> 3% of each run, Pallas kernels for 21% -> 21%
where the time goes in v3:
time: 44.2 us; the launch traced here: 43.4 us
  starting transfers between devices  19.7 us (45%)
  waiting for transfers between devices  11 us (25%)
  Pallas kernels  10.6 us (24%)
  local copies, waits for them, and re-layouts  1.28 us (3%)
  between operations  0.75 us (2%)
    ppermute x8, starting transfers between devices, exchange(): return lax.ppermute(value, axis, [(i, i ^ shift) for i in range(count)])  18.3 us
    ppermute x8, waiting for transfers between devices, exchange(): return lax.ppermute(value, axis, [(i, i ^ shift) for i in range(count)])  11 us
    pallas_call x1, Pallas kernels, per_device(): pl.pallas_call(main_kernel, out_shape=[jax.ShapeDtypeStruct((8, 128), jnp...  8.85 us
    ppermute x2, starting transfers between devices, per_device(): lax.ppermute(rows, 'narrow', across + ends)  1.39 us
    slice x1, local copies, waits for them, and re-layouts, per_device(): own[:half]  1.27 us
  transfers between devices with their start and end apart: 10, of which 6 were waited for; matrix products, arithmetic and copies ran while one was open for 3% of the time, Pallas kernels for 21%

profile of v3, /device:TPU:0, one launch (start us, length us, event | category | flops | bytes accessed | tf_op | source)
XLA Modules:
  0.0 43.4 jit_solution(5851342354628654401)
XLA Ops:
  0.6 0.0 copy-start.2
  0.6 0.0 copy-start.1
  0.7 0.0 copy-start
  0.7 0.5 %collective-permute-start = (f32[512,512]{1,0:T(8,128)}, f32[512,512]{1,0:T(8,128)S(1)}, u32[]{:S(2)}, u32[]{:S(2)}) collective-permute-start(f32[512,512]{1,0:T(8,128)} %bitcast.8), channel_id=1, source_target_pairs={{0,1},{1,0},{2,3},{3,2},{4,5},{5,4},{6,7},{7,6},{8,9},{9,8},{10,11... | collective-permute-start | bytes 3145736 | tf_op jit(solution)/shard_map/ppermute | solution.py:257
  1.2 1.3 %slice_bitcast_fusion = (f32[256,512]{1,0:T(8,128)S(1)}, f32[256,512]{1,0:T(8,128)S(1)}) fusion(f32[1,512,512]{2,1,0:T(8,128)} %state.1), kind=kLoop, calls=%fused_computation | loop fusion | bytes 2097152 | tf_op jit(solution)/shard_map/slice | solution.py:291
  2.4 0.7 %collective-permute-start.2 = (f32[256,512]{1,0:T(8,128)S(1)}, f32[256,512]{1,0:T(8,128)S(1)}, u32[]{:S(2)}, u32[]{:S(2)}) collective-permute-start(f32[256,512]{1,0:T(8,128)S(1)} %get-tuple-element.38), channel_id=1, source_target_pairs={{1,2},{2,1},{0,0},{3,3},{5,6},{6,5},{4,4},{7,7},{9,10},{10,9},{8,8... | collective-permute-start | bytes 1572872 | tf_op jit(solution)/shard_map/ppermute | solution.py:291
  3.2 0.7 %collective-permute-start.1 = (f32[256,512]{1,0:T(8,128)S(1)}, f32[256,512]{1,0:T(8,128)S(1)}, u32[]{:S(2)}, u32[]{:S(2)}) collective-permute-start(f32[256,512]{1,0:T(8,128)S(1)} %get-tuple-element.39), channel_id=1, source_target_pairs={{1,2},{2,1},{0,0},{3,3},{5,6},{6,5},{4,4},{7,7},{9,10},{10,9},{8,8... | collective-permute-start | bytes 1572872 | tf_op jit(solution)/shard_map/ppermute | solution.py:291
  3.9 0.0 collective-permute-done.near
  3.9 0.0 copy-done.2
  3.9 0.0 copy-done.1
  3.9 0.0 copy-done
  3.9 8.9 %main.1 = (s32[8,128]{1,0:T(8,128)S(1)}, f32[512,512]{1,0:T(8,128)S(1)}, f32[64,512]{1,0:T(8,128)S(1)}, f32[8,128]{1,0:T(8,128)S(1)}, bf16[4,512,512]{2,1,0:T(8,...) custom-call(s32[4]{0:T(128)S(1)} %copy-done, ...), custom_call_target="tpu_custom_call" | custom-call | flops 3221225472 | bytes 8388608 | tf_op jit(solution)/shard_map/main/pallas_call | solution.py:295
  12.8 0.0 collective-permute-done.2.far
  12.8 0.3 far.1.before
  13.1 0.0 collective-permute-done.1.far
  13.1 0.7 %last.1 = (f32[136,512]{1,0:T(8,128)S(1)}, f32[136,512]{1,0:T(8,128)S(1)}, f32[136,512]{1,0:T(8,128)S(1)}, f32[136,512]{1,0:T(8,128)S(1)}) custom-call(s32[8,128]{1,0:T(8,128)S(1)} %get-tuple-element.21.table, f32[256,512]{1,0:T(8,128)S(1)} %collective-permute-done.1.far, bf16[4,512,512]{2,1,0:T(8,128)(2,1)S(1)} %get-tuple-element.22.lh, ...), custom_call_target="tpu_custom_call" | custom-call | flops 3221225472 | bytes 1048576 | tf_op jit(solution)/shard_map/last/pallas_call | solution.py:329
  13.8 5.3 %collective-permute-start.3 = (f32[136,512]{1,0:T(8,128)S(1)}, f32[136,512]{1,0:T(8,128)S(1)}, u32[]{:S(2)}, u32[]{:S(2)}) collective-permute-start(f32[136,512]{1,0:T(8,128)S(1)} %get-tuple-element.30), channel_id=1, source_target_pairs={{0,12},{4,8},{8,4},{12,0},{16,28},{20,24},{24,20},{28,16},{1,13},{... | collective-permute-start | bytes 835592 | tf_op jit(solution)/shard_map/ppermute | solution.py:257
  19.1 0.0 collective-permute-start.4
  19.1 0.6 %collective-permute-start.5 = (f32[136,512]{1,0:T(8,128)S(1)}, f32[136,512]{1,0:T(8,128)S(1)}, u32[]{:S(2)}, u32[]{:S(2)}) collective-permute-start(f32[136,512]{1,0:T(8,128)S(1)} %get-tuple-element.32), channel_id=1, source_target_pairs={{0,4},{4,0},{8,12},{12,8},{16,20},{20,16},{24,28},{28,24},{1,5},{5... | collective-permute-start | bytes 835592 | tf_op jit(solution)/shard_map/ppermute | solution.py:257
  19.7 4.0 %collective-permute-done.3.refs_1_ = f32[136,512]{1,0:T(8,128)S(1)} collective-permute-done((f32[136,512]{1,0:T(8,128)S(1)}, f32[136,512]{1,0:T(8,128)S(1)}, u32[]{:S(2)}, u32[]{:S(2)}) %collective-permute-start.3) | collective-permute-done | bytes 278560 | tf_op jit(solution)/shard_map/ppermute | solution.py:257
  23.7 3.1 %collective-permute-done.4.refs_2_ = f32[136,512]{1,0:T(8,128)S(1)} collective-permute-done((f32[136,512]{1,0:T(8,128)S(1)}, f32[136,512]{1,0:T(8,128)S(1)}, u32[]{:S(2)}, u32[]{:S(2)}) %collective-permute-start.4) | collective-permute-done | bytes 278560 | tf_op jit(solution)/shard_map/ppermute | solution.py:257
  26.8 0.1 collective-permute-done.5.refs_3_
  26.9 0.1 merge.1
  27.0 1.3 %collective-permute-start.7 = (f32[8,128]{1,0:T(8,128)S(1)}, f32[8,128]{1,0:T(8,128)S(1)}, u32[]{:S(2)}, u32[]{:S(2)}) collective-permute-start(f32[8,128]{1,0:T(8,128)S(1)} %get-tuple-element.35.refs_0_), channel_id=1, source_target_pairs={{0,16},{4,20},{8,24},{12,28},{16,0},{20,4},{24,8},{28,12},{1,17},{... | collective-permute-start | bytes 12296 | tf_op jit(solution)/shard_map/ppermute | solution.py:257
  28.3 1.7 %collective-permute-start.6 = (f32[64,512]{1,0:T(8,128)S(1)}, f32[64,512]{1,0:T(8,128)S(1)}, u32[]{:S(2)}, u32[]{:S(2)}) collective-permute-start(f32[64,512]{1,0:T(8,128)S(1)} %get-tuple-element.34), channel_id=1, source_target_pairs={{0,16},{4,20},{8,24},{12,28},{16,0},{20,4},{24,8},{28,12},{1,17},{... | collective-permute-start | bytes 393224 | tf_op jit(solution)/shard_map/ppermute | solution.py:257
  30.0 1.7 %collective-permute-done.7.refs_1_ = f32[8,128]{1,0:T(8,128)S(1)} collective-permute-done((f32[8,128]{1,0:T(8,128)S(1)}, f32[8,128]{1,0:T(8,128)S(1)}, u32[]{:S(2)}, u32[]{:S(2)}) %collective-permute-start.7) | collective-permute-done | bytes 4128 | tf_op jit(solution)/shard_map/ppermute | solution.py:257
  31.7 5.3 %collective-permute-start.8 = (f32[8,128]{1,0:T(8,128)S(1)}, f32[8,128]{1,0:T(8,128)S(1)}, u32[]{:S(2)}, u32[]{:S(2)}) collective-permute-start(f32[8,128]{1,0:T(8,128)S(1)} %wide.1.refs_0_), channel_id=1, source_target_pairs={{0,1},{1,0},{2,3},{3,2},{4,5},{5,4},{6,7},{7,6},{8,9},{9,8},{10,11... | collective-permute-start | bytes 12296 | tf_op jit(solution)/shard_map/ppermute | solution.py:257
  37.0 0.8 %collective-permute-done.8.refs_1_ = f32[8,128]{1,0:T(8,128)S(1)} collective-permute-done((f32[8,128]{1,0:T(8,128)S(1)}, f32[8,128]{1,0:T(8,128)S(1)}, u32[]{:S(2)}, u32[]{:S(2)}) %collective-permute-start.8) | collective-permute-done | bytes 4128 | tf_op jit(solution)/shard_map/ppermute | solution.py:257
  37.8 3.6 %collective-permute-start.9 = (f32[8,128]{1,0:T(8,128)S(1)}, f32[8,128]{1,0:T(8,128)S(1)}, u32[]{:S(2)}, u32[]{:S(2)}) collective-permute-start(f32[8,128]{1,0:T(8,128)S(1)} %sectors.1.rest_2_), channel_id=1, source_target_pairs={{0,3},{1,2},{2,1},{3,0},{4,7},{5,6},{6,5},{7,4},{8,11},{9,10},{10,... | collective-permute-start | bytes 12296 | tf_op jit(solution)/shard_map/ppermute | solution.py:257
  41.4 1.3 %collective-permute-done.9.rest_3_ = f32[8,128]{1,0:T(8,128)S(1)} collective-permute-done((f32[8,128]{1,0:T(8,128)S(1)}, f32[8,128]{1,0:T(8,128)S(1)}, u32[]{:S(2)}, u32[]{:S(2)}) %collective-permute-start.9) | collective-permute-done | bytes 4128 | tf_op jit(solution)/shard_map/ppermute | solution.py:257
  42.7 0.0 collective-permute-done.6.rest_1_
  42.7 0.7 %final.1 = (f32[64,512]{1,0:T(8,128)}, f32[1,128]{1,0:T(1,128)}) custom-call(f32[64,512]{1,0:T(8,128)S(1)} %get-tuple-element.20.psi, f32[64,512]{1,0:T(8,128)S(1)} %get-tuple-element.33.rest_0_, f32[64,512]{1,0:T(8,128)S(1)} %collective-permute-done.6.rest_1_, f32[8,128]{1,0:T(8,128)S(1)} %sectors.1.rest_2_, f32[8,128]{1,0:T(8,128)S(1)} %collective-permute-done.9.rest_3_), custom_call_target="tpu_custom_call" | custom-call | tf_op jit(solution)/shard_map/final/pallas_call | solution.py:352
  (2 shorter events, 0.0 us)
Async XLA Ops:
  0.6 3.2 %copy-start.2 = (s32[4]{0:T(128)S(1)}, s32[4]{0:T(128)}, u32[]{:S(2)}) copy-start(s32[4]{0:T(128)} %charge.1) | copy-start | bytes 52
  0.6 3.2 %copy-start.1 = (s32[4]{0:T(128)S(1)}, s32[4]{0:T(128)}, u32[]{:S(2)}) copy-start(s32[4]{0:T(128)} %rsz.1) | copy-start | bytes 52
  0.7 3.2 %copy-start = (s32[4]{0:T(128)S(1)}, s32[4]{0:T(128)}, u32[]{:S(2)}) copy-start(s32[4]{0:T(128)} %lsz.1) | copy-start | bytes 52
  0.7 3.2 %collective-permute-start = (f32[512,512]{1,0:T(8,128)}, f32[512,512]{1,0:T(8,128)S(1)}, u32[]{:S(2)}, u32[]{:S(2)}) collective-permute-start(f32[512,512]{1,0:T(8,128)} %bitcast.8), channel_id=1, source_target_pairs={{0,1},{1,0},{2,3},{3,2},{4,5},{5,4},{6,7},{7,6},{8,9},{9,8},{10,11... | collective-permute-start | bytes 3145736 | tf_op jit(solution)/shard_map/ppermute | solution.py:257
  2.4 10.3 %collective-permute-start.2 = (f32[256,512]{1,0:T(8,128)S(1)}, f32[256,512]{1,0:T(8,128)S(1)}, u32[]{:S(2)}, u32[]{:S(2)}) collective-permute-start(f32[256,512]{1,0:T(8,128)S(1)} %get-tuple-element.38), channel_id=1, source_target_pairs={{1,2},{2,1},{0,0},{3,3},{5,6},{6,5},{4,4},{7,7},{9,10},{10,9},{8,8... | collective-permute-start | bytes 1572872 | tf_op jit(solution)/shard_map/ppermute | solution.py:291
  3.2 10.0 %collective-permute-start.1 = (f32[256,512]{1,0:T(8,128)S(1)}, f32[256,512]{1,0:T(8,128)S(1)}, u32[]{:S(2)}, u32[]{:S(2)}) collective-permute-start(f32[256,512]{1,0:T(8,128)S(1)} %get-tuple-element.39), channel_id=1, source_target_pairs={{1,2},{2,1},{0,0},{3,3},{5,6},{6,5},{4,4},{7,7},{9,10},{10,9},{8,8... | collective-permute-start | bytes 1572872 | tf_op jit(solution)/shard_map/ppermute | solution.py:291
  13.8 9.9 %collective-permute-start.3 = (f32[136,512]{1,0:T(8,128)S(1)}, f32[136,512]{1,0:T(8,128)S(1)}, u32[]{:S(2)}, u32[]{:S(2)}) collective-permute-start(f32[136,512]{1,0:T(8,128)S(1)} %get-tuple-element.30), channel_id=1, source_target_pairs={{0,12},{4,8},{8,4},{12,0},{16,28},{20,24},{24,20},{28,16},{1,13},{... | collective-permute-start | bytes 835592 | tf_op jit(solution)/shard_map/ppermute | solution.py:257
  19.1 7.7 %collective-permute-start.4 = (f32[136,512]{1,0:T(8,128)S(1)}, f32[136,512]{1,0:T(8,128)S(1)}, u32[]{:S(2)}, u32[]{:S(2)}) collective-permute-start(f32[136,512]{1,0:T(8,128)S(1)} %get-tuple-element.31), channel_id=1, source_target_pairs={{0,8},{4,12},{8,0},{12,4},{16,24},{20,28},{24,16},{28,20},{1,9},{5... | collective-permute-start | bytes 835592 | tf_op jit(solution)/shard_map/ppermute | solution.py:257
  19.1 7.8 %collective-permute-start.5 = (f32[136,512]{1,0:T(8,128)S(1)}, f32[136,512]{1,0:T(8,128)S(1)}, u32[]{:S(2)}, u32[]{:S(2)}) collective-permute-start(f32[136,512]{1,0:T(8,128)S(1)} %get-tuple-element.32), channel_id=1, source_target_pairs={{0,4},{4,0},{8,12},{12,8},{16,20},{20,16},{24,28},{28,24},{1,5},{5... | collective-permute-start | bytes 835592 | tf_op jit(solution)/shard_map/ppermute | solution.py:257
  27.0 4.7 %collective-permute-start.7 = (f32[8,128]{1,0:T(8,128)S(1)}, f32[8,128]{1,0:T(8,128)S(1)}, u32[]{:S(2)}, u32[]{:S(2)}) collective-permute-start(f32[8,128]{1,0:T(8,128)S(1)} %get-tuple-element.35.refs_0_), channel_id=1, source_target_pairs={{0,16},{4,20},{8,24},{12,28},{16,0},{20,4},{24,8},{28,12},{1,17},{... | collective-permute-start | bytes 12296 | tf_op jit(solution)/shard_map/ppermute | solution.py:257
  28.3 14.5 %collective-permute-start.6 = (f32[64,512]{1,0:T(8,128)S(1)}, f32[64,512]{1,0:T(8,128)S(1)}, u32[]{:S(2)}, u32[]{:S(2)}) collective-permute-start(f32[64,512]{1,0:T(8,128)S(1)} %get-tuple-element.34), channel_id=1, source_target_pairs={{0,16},{4,20},{8,24},{12,28},{16,0},{20,4},{24,8},{28,12},{1,17},{... | collective-permute-start | bytes 393224 | tf_op jit(solution)/shard_map/ppermute | solution.py:257
  31.7 6.1 %collective-permute-start.8 = (f32[8,128]{1,0:T(8,128)S(1)}, f32[8,128]{1,0:T(8,128)S(1)}, u32[]{:S(2)}, u32[]{:S(2)}) collective-permute-start(f32[8,128]{1,0:T(8,128)S(1)} %wide.1.refs_0_), channel_id=1, source_target_pairs={{0,1},{1,0},{2,3},{3,2},{4,5},{5,4},{6,7},{7,6},{8,9},{9,8},{10,11... | collective-permute-start | bytes 12296 | tf_op jit(solution)/shard_map/ppermute | solution.py:257
  37.8 4.9 %collective-permute-start.9 = (f32[8,128]{1,0:T(8,128)S(1)}, f32[8,128]{1,0:T(8,128)S(1)}, u32[]{:S(2)}, u32[]{:S(2)}) collective-permute-start(f32[8,128]{1,0:T(8,128)S(1)} %sectors.1.rest_2_), channel_id=1, source_target_pairs={{0,3},{1,2},{2,1},{3,0},{4,7},{5,6},{6,5},{7,4},{8,11},{9,10},{10,... | collective-permute-start | bytes 12296 | tf_op jit(solution)/shard_map/ppermute | solution.py:257
